TPU v7x, 512 devices: a whole 4x8x8 slice. The times are simulated.
512 devices in a mesh: patch: 128 (over z, y, core), mp: 4 (over x).
Axes of the slice: x: 4, y: 8, z: 8, core: 2. Of those that a mesh axis runs over, the one named last changes fastest.
Arguments:
- points: bfloat16 [65536, 256], P(('patch', 'mp')), may hold values from -6 to 6
- patch_counts: int32 [128], replicated, may hold values from 256 to 512, as said below
- to_hilbert: int32 [65536], P('patch'), may hold values from 0 to 65535, as said below
- from_hilbert: int32 [65536], P('patch'), may hold values from 0 to 65535, as said below
- cotangent: bfloat16 [65536, 256], P(('patch', 'mp')), may hold values from -0.0625 to 0.0625
- gain_mixer: float32 [2, 256], replicated, may hold values from 0.5 to 1.5
- query_weight: bfloat16 [2, 256, 256], replicated, may hold values from -0.375 to 0.375
- key_weight: bfloat16 [2, 256, 256], replicated, may hold values from -0.375 to 0.375
- value_weight: bfloat16 [2, 256, 256], replicated, may hold values from -0.375 to 0.375
- out_weight: bfloat16 [2, 256, 256], replicated, may hold values from -0.375 to 0.375
- gain_feed: float32 [2, 256], replicated, may hold values from 0.5 to 1.5
- up_weight: bfloat16 [2, 256, 1024], replicated, may hold values from -0.375 to 0.375
- down_weight: bfloat16 [2, 1024, 256], replicated, may hold values from -0.1875 to 0.1875
Outputs:
- hilbert_out: bfloat16 [65536, 256], P(('patch', 'mp'))
- grad_gain_mixer: float32 [2, 256], replicated
- grad_query: float32 [2, 256, 256], P(None, 'mp')
- grad_key: float32 [2, 256, 256], P(None, 'mp')
- grad_value: float32 [2, 256, 256], P(None, 'mp')
- grad_out: float32 [2, 256, 256], P(None, 'mp')
- grad_gain_feed: float32 [2, 256], replicated
- grad_up: float32 [2, 256, 1024], P(None, 'mp')
- grad_down: float32 [2, 1024, 256], P(None, 'mp')
Inputs may be any that keep to these rules, and one draw needn't show every extreme that they name: z-ordered patch i holds points in its first patch_counts[i] rows and padding in the rest. A permutation of the rows: z-ordered row r becomes Hilbert row to_hilbert[r]; of the 512 rows of one aligned block, at most 6 land in any one aligned block of 512 rows, and some pair of blocks reaches 6. `from_hilbert`: the inverse permutation of to_hilbert.
All inputs are finite; a program needn't handle non-finite values.
Results may differ from a plain program's by a relative error of at most 0.034.
Values may be sent and summed in bfloat16 or wider, within the bound.
No kernel may reach another device: no remote copies, remote signals or barrier semaphores. Data moves between devices by JAX's collectives and lax.ppermute only.
A program may use at most 64 MiB of HBM per device.

v0:
```python
import jax
import jax.numpy as jnp
from jax import lax
from jax.sharding import PartitionSpec as P

HEADS = 16
PATCH = 512
HEAD_DIM = 16


EPSILON = 1e-05
GELU_SCALE = 0.7978845608028654
GELU_CUBIC = 0.044715


def norm_rows(values, gain_row):
    widened = values.astype(jnp.float32)
    centered = widened - jnp.mean(widened, axis=1, keepdims=True)
    inverse = lax.rsqrt(jnp.mean(centered * centered, axis=1, keepdims=True) + EPSILON)
    normed = centered * inverse
    return (normed, inverse, (normed * gain_row[None, :]).astype(jnp.bfloat16))


def norm_back(grad_scaled, normed, inverse, gain_row):
    grad_gain = jnp.sum(grad_scaled * normed, axis=0)
    grad_normed = grad_scaled * gain_row[None, :]
    centered = grad_normed - jnp.mean(grad_normed, axis=1, keepdims=True)
    return (
        grad_gain,
        inverse * (centered - normed * jnp.mean(grad_normed * normed, axis=1, keepdims=True)),
    )


def gelu_pair(pre_act):
    cubed_part = pre_act * pre_act * pre_act
    tangent = jnp.tanh(GELU_SCALE * (pre_act + GELU_CUBIC * cubed_part))
    activated = 0.5 * pre_act * (1.0 + tangent)
    slopes = 0.5 * (1.0 + tangent) + 0.5 * pre_act * (1.0 - tangent * tangent) * GELU_SCALE * (
        1.0 + 3.0 * GELU_CUBIC * pre_act * pre_act
    )
    return (activated, slopes)


def patch_frame(row_count):
    group_rows = min(row_count, PATCH)
    group_patches = row_count // group_rows
    first_row = lax.axis_index("mp") * row_count
    return (group_rows, group_patches, first_row // PATCH, first_row % PATCH)


def own_patches(block_matrix):
    shaped = block_matrix.reshape(block_matrix.shape[0] // PATCH, PATCH, block_matrix.shape[1])
    return shaped


def allowed_keys(live_block, frame):
    group_rows, group_patches, first_patch, offset = frame
    live_grid = live_block.reshape(live_block.shape[0] // PATCH, PATCH)
    row_ids = lax.broadcasted_iota(jnp.int32, (group_rows, PATCH), 0) + offset
    col_ids = lax.broadcasted_iota(jnp.int32, (group_rows, PATCH), 1)
    return (live_grid[:, None, :] > 0) | (row_ids == col_ids)[None, :, :]


def split_heads(patched):
    return patched.reshape(patched.shape[0], patched.shape[1], HEADS, HEAD_DIM).transpose(
        2, 0, 1, 3
    )


def join_heads(stacked):
    head_count, patches, rows = (stacked.shape[0], stacked.shape[1], stacked.shape[2])
    return stacked.transpose(1, 2, 0, 3).reshape(patches * rows, head_count * HEAD_DIM)


def head_probability(query_head, key_head, allowed):
    scores = jnp.einsum(
        "npd,nkd->npk", query_head, key_head, preferred_element_type=jnp.float32
    ) * HEAD_DIM ** (-0.5)
    weights = jnp.where(allowed, jnp.exp(scores), 0.0)
    return weights / jnp.sum(weights, axis=2, keepdims=True)


def attend(query_m, key_patches, value_patches, allowed, frame):
    group_rows, group_patches, first_patch, offset = frame

    def one_head(operands):
        query_head, key_head, value_head = operands
        probability = head_probability(query_head, key_head, allowed)
        return jnp.einsum(
            "npk,nkd->npd",
            probability.astype(jnp.bfloat16),
            value_head,
            preferred_element_type=jnp.float32,
        ).astype(jnp.bfloat16)

    query_patches = query_m.reshape(group_patches, group_rows, query_m.shape[1])
    return join_heads(
        lax.map(
            one_head,
            (split_heads(query_patches), split_heads(key_patches), split_heads(value_patches)),
        )
    )


def attend_back(query_m, key_patches, value_patches, grad_heads, allowed, frame):
    group_rows, group_patches, first_patch, offset = frame

    def one_head(operands):
        query_head, key_head, value_head, grad_head = operands
        probability = head_probability(query_head, key_head, allowed)
        grad_prob = jnp.einsum(
            "npd,nkd->npk", grad_head, value_head, preferred_element_type=jnp.float32
        )
        value_term = jnp.einsum(
            "npk,npd->nkd",
            probability.astype(jnp.bfloat16),
            grad_head,
            preferred_element_type=jnp.float32,
        )
        inner_sum = jnp.sum(probability * grad_prob, axis=2, keepdims=True)
        grad_score = (probability * (grad_prob - inner_sum) * HEAD_DIM ** (-0.5)).astype(
            jnp.bfloat16
        )
        grad_query = jnp.einsum(
            "npk,nkd->npd", grad_score, key_head, preferred_element_type=jnp.float32
        ).astype(jnp.bfloat16)
        key_term = jnp.einsum(
            "npk,npd->nkd", grad_score, query_head, preferred_element_type=jnp.float32
        )
        return (grad_query, key_term, value_term)

    query_patches = query_m.reshape(group_patches, group_rows, query_m.shape[1])
    grad_patches = grad_heads.reshape(group_patches, group_rows, grad_heads.shape[1])
    results = lax.map(
        one_head,
        (
            split_heads(query_patches),
            split_heads(key_patches),
            split_heads(value_patches),
            split_heads(grad_patches),
        ),
    )
    return (join_heads(results[0]), join_heads(results[1]), join_heads(results[2]))


def contract_rows(left_rows, right_rows):
    return lax.dot_general(
        left_rows, right_rows, (((0,), (0,)), ((), ())), preferred_element_type=jnp.float32
    )


def contract_columns(left_rows, right_rows):
    return lax.dot_general(
        left_rows, right_rows, (((1,), (1,)), ((), ())), preferred_element_type=jnp.float32
    )


def bucket_slots(owners, ranking, peer_count):
    local_rows = owners.shape[0]
    sort_keys = owners * local_rows + ranking
    position = jnp.argsort(jnp.argsort(sort_keys))
    member = (owners[:, None] == jnp.arange(peer_count, dtype=jnp.int32)[None, :]).astype(jnp.int32)
    totals = jnp.sum(member, axis=0)
    starts = jnp.cumsum(totals) - totals
    group_start = jnp.sum(member * starts[None, :], axis=1)
    return position - group_start


def ship_rows(full_rows, pack_owner, pack_slot, take_owner, take_slot, capacity):
    peer_count = lax.axis_size("patch")
    buffer_rows = jnp.zeros((peer_count, capacity, full_rows.shape[1]), full_rows.dtype)
    buffer_rows = buffer_rows.at[pack_owner, pack_slot].set(full_rows)
    arrived = lax.all_to_all(buffer_rows, "patch", split_axis=0, concat_axis=0, tiled=True)
    return arrived[take_owner, take_slot]


def move_rows(quarter_block, pack_owner, pack_slot, take_owner, take_slot, capacity):
    full_rows = lax.all_gather(quarter_block, "mp", axis=0, tiled=True)
    moved = ship_rows(full_rows, pack_owner, pack_slot, take_owner, take_slot, capacity)
    result = lax.dynamic_slice_in_dim(
        moved, lax.axis_index("mp") * quarter_block.shape[0], quarter_block.shape[0], 0
    )
    return result


def block_forward(rows_in, live_block, params):
    (
        gain_mixer,
        query_weight,
        key_weight,
        value_weight,
        out_weight,
        gain_feed,
        up_weight,
        down_weight,
    ) = params
    frame = patch_frame(rows_in.shape[0])
    allowed = allowed_keys(live_block, frame)
    normed_a, inverse_a, scaled_a = norm_rows(rows_in, gain_mixer)
    width = query_weight.shape[1]
    joined_weight = jnp.concatenate([query_weight, key_weight, value_weight], axis=1)
    projected = jnp.dot(scaled_a, joined_weight, preferred_element_type=jnp.float32).astype(
        jnp.bfloat16
    )
    query_m = projected[:, :width]
    key_m = projected[:, width : 2 * width]
    value_m = projected[:, 2 * width :]
    full_key, full_value = (
        lax.all_gather(key_m, "mp", axis=0, tiled=True),
        lax.all_gather(value_m, "mp", axis=0, tiled=True),
    )
    key_patches = own_patches(full_key)
    value_patches = own_patches(full_value)
    heads_out = attend(query_m, key_patches, value_patches, allowed, frame)
    middle = (
        rows_in.astype(jnp.float32)
        + jnp.dot(heads_out, out_weight, preferred_element_type=jnp.float32)
    ).astype(jnp.bfloat16)
    normed_m, inverse_m, scaled_m = norm_rows(middle, gain_feed)
    activated, slopes = gelu_pair(jnp.dot(scaled_m, up_weight, preferred_element_type=jnp.float32))
    hidden = activated.astype(jnp.bfloat16)
    block_out = (
        middle.astype(jnp.float32)
        + jnp.dot(hidden, down_weight, preferred_element_type=jnp.float32)
    ).astype(jnp.bfloat16)
    kept_state = (
        normed_a,
        inverse_a,
        scaled_a,
        query_m,
        key_patches,
        value_patches,
        heads_out,
        normed_m,
        inverse_m,
        scaled_m,
        slopes,
        hidden,
    )
    return (block_out, kept_state)


def block_backward(grad_rows, kept_state, params, live_block):
    (
        gain_mixer,
        query_weight,
        key_weight,
        value_weight,
        out_weight,
        gain_feed,
        up_weight,
        down_weight,
    ) = params
    (
        normed_a,
        inverse_a,
        scaled_a,
        query_m,
        key_patches,
        value_patches,
        heads_out,
        normed_m,
        inverse_m,
        scaled_m,
        slopes,
        hidden,
    ) = kept_state
    row_count = grad_rows.shape[0]
    frame = patch_frame(row_count)
    allowed = allowed_keys(live_block, frame)
    down_grad = contract_rows(hidden, grad_rows)
    grad_pre = (contract_columns(grad_rows, down_weight) * slopes).astype(jnp.bfloat16)
    up_grad = contract_rows(scaled_m, grad_pre)
    grad_scaled_m = contract_columns(grad_pre, up_weight)
    feed_gain_grad, grad_middle_norm = norm_back(grad_scaled_m, normed_m, inverse_m, gain_feed)
    grad_middle = (grad_rows.astype(jnp.float32) + grad_middle_norm).astype(jnp.bfloat16)
    out_grad = contract_rows(heads_out, grad_middle)
    grad_heads = contract_columns(grad_middle, out_weight).astype(jnp.bfloat16)
    grad_query, key_term, value_term = attend_back(
        query_m, key_patches, value_patches, grad_heads, allowed, frame
    )
    key_sums, value_sums = (
        lax.psum_scatter(
            key_term.astype(jnp.bfloat16), "mp", scatter_dimension=0, tiled=True
        ).astype(jnp.float32),
        lax.psum_scatter(
            value_term.astype(jnp.bfloat16), "mp", scatter_dimension=0, tiled=True
        ).astype(jnp.float32),
    )
    grad_key = key_sums.astype(jnp.bfloat16)
    grad_value = value_sums.astype(jnp.bfloat16)
    query_grad = contract_rows(scaled_a, grad_query)
    key_grad = contract_rows(scaled_a, grad_key)
    value_grad = contract_rows(scaled_a, grad_value)
    joined_grad = jnp.concatenate([grad_query, grad_key, grad_value], axis=1)
    joined_weight = jnp.concatenate([query_weight, key_weight, value_weight], axis=1)
    grad_scaled_a = contract_columns(joined_grad, joined_weight)
    mixer_gain_grad, grad_in_norm = norm_back(grad_scaled_a, normed_a, inverse_a, gain_mixer)
    grad_in = (grad_middle.astype(jnp.float32) + grad_in_norm).astype(jnp.bfloat16)
    return (
        (query_grad, key_grad, value_grad, out_grad, up_grad, down_grad),
        (mixer_gain_grad, feed_gain_grad),
        grad_in,
    )


def split_rows(grads, mp_size):
    return tuple(
        (single.reshape(mp_size, single.shape[0] // mp_size, single.shape[1]) for single in grads)
    )


def fold_terms(arrived):
    return tuple((jnp.sum(single, axis=0) for single in arrived))


def body(
    points,
    patch_counts,
    to_hilbert,
    from_hilbert,
    cotangent,
    gain_mixer,
    query_weight,
    key_weight,
    value_weight,
    out_weight,
    gain_feed,
    up_weight,
    down_weight,
):
    local_rows = to_hilbert.shape[0]
    peer_count = lax.axis_size("patch")
    mp_size = lax.axis_size("mp")
    capacity = 3 * (local_rows // peer_count) // 2
    local_patches = local_rows // PATCH
    own_counts = lax.dynamic_slice_in_dim(
        patch_counts, lax.axis_index("patch") * local_patches, local_patches, 0
    )
    live_zorder = (
        (jnp.arange(PATCH, dtype=jnp.int32)[None, :] < own_counts[:, None])
        .astype(jnp.int32)
        .reshape(local_rows)
    )
    source_patch = from_hilbert // PATCH
    table_match = (
        source_patch[:, None] == jnp.arange(patch_counts.shape[0], dtype=jnp.int32)[None, :]
    )
    source_count = jnp.sum(jnp.where(table_match, patch_counts[None, :], 0), axis=1)
    live_hilbert = (from_hilbert % PATCH < source_count).astype(jnp.int32)
    position = jnp.arange(local_rows, dtype=jnp.int32)
    depart_owner = to_hilbert // local_rows
    depart_slot = bucket_slots(depart_owner, position, peer_count)
    arrive_owner = from_hilbert // local_rows
    arrive_slot = bucket_slots(arrive_owner, from_hilbert % local_rows, peer_count)
    stacks = (
        gain_mixer,
        query_weight,
        key_weight,
        value_weight,
        out_weight,
        gain_feed,
        up_weight,
        down_weight,
    )
    first_params = tuple((stacked[0] for stacked in stacks))
    second_params = tuple((stacked[1] for stacked in stacks))
    first_out, first_state = block_forward(points, live_zorder, first_params)
    second_in = move_rows(first_out, depart_owner, depart_slot, arrive_owner, arrive_slot, capacity)
    second_out, second_state = block_forward(second_in, live_hilbert, second_params)
    second_grads, second_gains, grad_second_in = block_backward(
        cotangent, second_state, second_params, live_hilbert
    )
    grad_first_out = move_rows(
        grad_second_in, arrive_owner, arrive_slot, depart_owner, depart_slot, capacity
    )
    first_grads, first_gains, unused_grad = block_backward(
        grad_first_out, first_state, first_params, live_zorder
    )
    fq, fk, fv, fo, fu, fd = split_rows(first_grads, mp_size)
    sq, sk, sv, so, su, sd = split_rows(second_grads, mp_size)
    arrived_all = (
        lax.all_to_all(
            fq.astype(jnp.bfloat16), "mp", split_axis=0, concat_axis=0, tiled=True
        ).astype(fq.dtype),
        lax.all_to_all(
            fk.astype(jnp.bfloat16), "mp", split_axis=0, concat_axis=0, tiled=True
        ).astype(fk.dtype),
        lax.all_to_all(
            fv.astype(jnp.bfloat16), "mp", split_axis=0, concat_axis=0, tiled=True
        ).astype(fv.dtype),
        lax.all_to_all(
            fo.astype(jnp.bfloat16), "mp", split_axis=0, concat_axis=0, tiled=True
        ).astype(fo.dtype),
        lax.all_to_all(
            fu.astype(jnp.bfloat16), "mp", split_axis=0, concat_axis=0, tiled=True
        ).astype(fu.dtype),
        lax.all_to_all(
            fd.astype(jnp.bfloat16), "mp", split_axis=0, concat_axis=0, tiled=True
        ).astype(fd.dtype),
        lax.all_to_all(
            sq.astype(jnp.bfloat16), "mp", split_axis=0, concat_axis=0, tiled=True
        ).astype(sq.dtype),
        lax.all_to_all(
            sk.astype(jnp.bfloat16), "mp", split_axis=0, concat_axis=0, tiled=True
        ).astype(sk.dtype),
        lax.all_to_all(
            sv.astype(jnp.bfloat16), "mp", split_axis=0, concat_axis=0, tiled=True
        ).astype(sv.dtype),
        lax.all_to_all(
            so.astype(jnp.bfloat16), "mp", split_axis=0, concat_axis=0, tiled=True
        ).astype(so.dtype),
        lax.all_to_all(
            su.astype(jnp.bfloat16), "mp", split_axis=0, concat_axis=0, tiled=True
        ).astype(su.dtype),
        lax.all_to_all(
            sd.astype(jnp.bfloat16), "mp", split_axis=0, concat_axis=0, tiled=True
        ).astype(sd.dtype),
    )
    uq, uk, uv, uo, uu, ud, tq, tk, tv, to_sum, tu, td = fold_terms(arrived_all)
    all_sums = lax.psum((uq, uk, uv, uo, uu, ud, tq, tk, tv, to_sum, tu, td), "patch")
    first_sums = all_sums[:6]
    second_sums = all_sums[6:]
    mixer_gains, feed_gains = lax.psum(
        (
            jnp.stack([first_gains[0], second_gains[0]]),
            jnp.stack([first_gains[1], second_gains[1]]),
        ),
        ("patch", "mp"),
    )
    stacked = [jnp.stack([first_sums[member], second_sums[member]]) for member in range(6)]
    return (
        second_out,
        mixer_gains,
        stacked[0],
        stacked[1],
        stacked[2],
        stacked[3],
        feed_gains,
        stacked[4],
        stacked[5],
    )


def solution(mesh):
    in_specs = (
        P(("patch", "mp"), None),
        P(),
        P("patch"),
        P("patch"),
        P(("patch", "mp"), None),
        P(),
        P(),
        P(),
        P(),
        P(),
        P(),
        P(),
        P(),
    )
    out_specs = (
        P(("patch", "mp"), None),
        P(),
        P(None, "mp", None),
        P(None, "mp", None),
        P(None, "mp", None),
        P(None, "mp", None),
        P(),
        P(None, "mp", None),
        P(None, "mp", None),
    )
    return jax.shard_map(body, mesh=mesh, in_specs=in_specs, out_specs=out_specs, check_vma=False)
```

profile of v0, /device:TPU:1, one launch (start us, length us, event | category | flops | bytes accessed | tf_op | source)
XLA Modules:
  0.0 742.9 jit_solution(11479298185214731768)
XLA Ops:
  11.9 10.5 %all_gather.18 = bf16[512,256]{1,0:T(8,128)(2,1)S(1)} all-gather(bf16[128,256]{1,0:T(8,128)(2,1)S(1)} %get-tuple-element.493), channel_id=1, replica_groups=mesh['patch'=128,'mp'=4] {'mp'}, dimensions={0}, use_global_device_ids=true | all-gather | bytes 327680 | tf_op jit(solution)/shard_map/all_gather | solution.py:209
  22.6 9.4 %all_gather.19 = bf16[512,256]{1,0:T(8,128)(2,1)S(1)} all-gather(bf16[128,256]{1,0:T(8,128)(2,1)S(1)} %get-tuple-element.492), channel_id=1, replica_groups=mesh['patch'=128,'mp'=4] {'mp'}, dimensions={0}, use_global_device_ids=true | all-gather | bytes 327680 | tf_op jit(solution)/shard_map/all_gather | solution.py:210
  34.1 9.1 %while.52 = (s32[]{:T(128)}, bf16[16,1,128,16]{2,3,1,0:T(8,128)(2,1)S(1)}, bf16[16,1,128,16]{2,3,1,0:T(8,128)(2,1)S(1)}, bf16[16,1,512,16]{2,3,1,0:T(8,128)(2,1)...) while((s32[]{:T(128)}, ...), condition=%wide.region_9.10_spmd.clone, body=%wide.region_7.9_spmd.clone.sunk | while | flops 4654978 | bytes 569429 | solution.py:98
  46.7 9.4 %all_gather.20 = bf16[512,256]{1,0:T(8,128)(2,1)S(1)} all-gather(bf16[128,256]{1,0:T(8,128)(2,1)S(1)} %fusion.96), channel_id=1, replica_groups=mesh['patch'=128,'mp'=4] {'mp'}, dimensions={0}, use_global_device_ids=true | all-gather | bytes 327680 | tf_op jit(solution)/shard_map/all_gather | solution.py:178
  64.4 25.3 %scatter_fusion = bf16[128,6,256]{2,0,1:T(8,128)(2,1)S(1)} fusion(bf16[128,6,256]{2,0,1:T(8,128)(2,1)S(1)} %broadcast.300.clone, s32[512]{0:T(512)S(1)} %bitcast.404, bf16[512,256]{1,0:T(8,128)(2,1)S(1)} %all_gather.20), kind=kCustom, calls=%fused_computation.2 | custom fusion | bytes 790528 | tf_op jit(solution)/shard_map/scatter | solution.py:172
  90.8 26.3 %all-to-all-start = ((bf16[128,6,256]{2,1,0:T(8,128)(2,1)}), bf16[128,6,256]{2,1,0:T(8,128)(2,1)S(1)}, u32[]{:S(2)}, u32[]{:S(2)}) async-start(bf16[128,6,256]{2,1,0:T(8,128)(2,1)} %copy.103), calls=%async_computation | async-start | bytes 1048576 | tf_op jit(solution)/shard_map/all_to_all | solution.py:173
  125.6 12.0 %all-to-all-done = bf16[128,6,256]{2,1,0:T(8,128)(2,1)S(1)} async-done(((bf16[128,6,256]{2,1,0:T(8,128)(2,1)}), bf16[128,6,256]{2,1,0:T(8,128)(2,1)S(1)}, u32[]{:S(2)}, u32[]{:S(2)}) %all-to-all-start) | async-done | bytes 393248 | tf_op jit(solution)/shard_map/all_to_all | solution.py:173
  142.0 10.0 %all_gather.21 = bf16[512,256]{1,0:T(8,128)(2,1)S(1)} all-gather(bf16[128,256]{1,0:T(8,128)(2,1)S(1)} %get-tuple-element.490), channel_id=1, replica_groups=mesh['patch'=128,'mp'=4] {'mp'}, dimensions={0}, use_global_device_ids=true | all-gather | bytes 327680 | tf_op jit(solution)/shard_map/all_gather | solution.py:209
  152.1 9.4 %all_gather.22 = bf16[512,256]{1,0:T(8,128)(2,1)S(1)} all-gather(bf16[128,256]{1,0:T(8,128)(2,1)S(1)} %get-tuple-element.489), channel_id=1, replica_groups=mesh['patch'=128,'mp'=4] {'mp'}, dimensions={0}, use_global_device_ids=true | all-gather | bytes 327680 | tf_op jit(solution)/shard_map/all_gather | solution.py:210
  161.8 9.1 %while.53 = (s32[]{:T(128)}, bf16[16,1,128,16]{2,3,1,0:T(8,128)(2,1)S(1)}, bf16[16,1,128,16]{2,3,1,0:T(8,128)(2,1)S(1)}, bf16[16,1,512,16]{2,3,1,0:T(8,128)(2,1)...) while((s32[]{:T(128)}, ...), condition=%wide.region_23.24_spmd.clone, body=%wide.region_21.23_spmd.clone.sunk | while | flops 4654978 | bytes 569429 | solution.py:98
  175.5 53.6 %while.54 = (s32[]{:T(128)}, bf16[16,1,128,16]{2,3,1,0:T(8,128)(2,1)S(1)}, bf16[16,1,512,16]{2,3,1,0:T(8,128)(2,1)S(1)}, bf16[16,1,512,16]{2,3,1,0:T(8,128)(2,1)...) while((s32[]{:T(128)}, ...), condition=%wide.region_31.32_spmd.clone, body=%wide.region_28.31_spmd.clone.sunk | while | flops 11470594 | bytes 2114725 | solution.py:134
  246.1 5.1 all-to-all-done.11
  256.5 24.1 %reduce-scatter.15.cloned.1.call-done = bf16[128,256]{1,0:T(8,128)(2,1)} async-done(((bf16[512,256]{1,0:T(8,128)(2,1)}), bf16[128,256]{1,0:T(8,128)(2,1)}) %reduce-scatter.15.cloned.1.call-update) | async-done | bytes 65552
  283.6 9.4 %all_gather.23 = bf16[512,256]{1,0:T(8,128)(2,1)S(1)} all-gather(bf16[128,256]{1,0:T(8,128)(2,1)S(1)} %fusion.163), channel_id=1, replica_groups=mesh['patch'=128,'mp'=4] {'mp'}, dimensions={0}, use_global_device_ids=true | all-gather | bytes 327680 | tf_op jit(solution)/shard_map/all_gather | solution.py:178
  293.0 25.3 %scatter_fusion.1 = bf16[128,6,256]{2,0,1:T(8,128)(2,1)S(1)} fusion(bf16[128,6,256]{2,0,1:T(8,128)(2,1)S(1)} %broadcast.300, s32[512]{0:T(512)S(1)} %bitcast.402, bf16[512,256]{1,0:T(8,128)(2,1)S(1)} %all_gather.23), kind=kCustom, calls=%fused_computation.3 | custom fusion | bytes 790528 | tf_op jit(solution)/shard_map/scatter | solution.py:172
  319.3 19.4 %all-to-all-start.1 = ((bf16[128,6,256]{2,1,0:T(8,128)(2,1)}), bf16[128,6,256]{2,1,0:T(8,128)(2,1)S(1)}, u32[]{:S(2)}, u32[]{:S(2)}) async-start(bf16[128,6,256]{2,1,0:T(8,128)(2,1)} %copy.117), calls=%async_computation.1 | async-start | bytes 1048576 | tf_op jit(solution)/shard_map/all_to_all | solution.py:173
  343.0 16.2 %all-to-all-done.1 = bf16[128,6,256]{2,1,0:T(8,128)(2,1)S(1)} async-done(((bf16[128,6,256]{2,1,0:T(8,128)(2,1)}), bf16[128,6,256]{2,1,0:T(8,128)(2,1)S(1)}, u32[]{:S(2)}, u32[]{:S(2)}) %all-to-all-start.1) | async-done | bytes 393248 | tf_op jit(solution)/shard_map/all_to_all | solution.py:173
  368.4 4.2 all-to-all-start.5
  373.2 65.5 %while.55 = (s32[]{:T(128)}, bf16[16,1,128,16]{2,3,1,0:T(8,128)(2,1)S(1)}, bf16[16,1,512,16]{2,3,1,0:T(8,128)(2,1)S(1)}, bf16[16,1,512,16]{2,3,1,0:T(8,128)(2,1)...) while((s32[]{:T(128)}, ...), condition=%wide.region_42.43_spmd.clone, body=%wide.region_39.42_spmd.clone.sunk | while | flops 11470594 | bytes 2110573 | solution.py:134
  438.8 4.2 all-to-all-start.3
  491.2 21.1 %reduce-scatter.19.cloned.1.call-done = bf16[128,256]{1,0:T(8,128)(2,1)} async-done(((bf16[512,256]{1,0:T(8,128)(2,1)}), bf16[128,256]{1,0:T(8,128)(2,1)}) %reduce-scatter.19.cloned.1.call-update) | async-done | bytes 65552
  518.1 4.1 all-to-all-done.6
  527.5 101.3 %all-reduce = (f32[2,256]{1,0:T(2,128)}, f32[2,256]{1,0:T(2,128)}) all-reduce(f32[2,256]{1,0:T(2,128)S(1)} %pad_maximum_fusion.12, f32[2,256]{1,0:T(2,128)S(1)} %pad_maximum_fusion.13), channel_id=1, replica_groups=mesh['patch'=128,'mp'=4] {'patch','mp'}, use_global_device_ids=true, to_apply=%region_47.48 | all-reduce | flops 1024 | bytes 8192 | tf_op jit(solution)/shard_map/psum | solution.py:424
  628.8 101.4 %all-reduce.4.cloned.1.call-done = (f32[1,64,256]{2,1,0:T(8,128)}, f32[1,64,256]{2,1,0:T(8,128)}, f32[1,64,256]{2,1,0:T(8,128)}, f32[1,64,256]{2,1,0:T(8,128)}, ...) async-done(((f32[1,64,256]{2,1,0:T(8,128)}, ...) | async-done | bytes 1572880 | tf_op jit(solution)/shard_map/psum | solution.py:421
  (655 shorter events, 279.0 us)
Async XLA Ops:
  10.9 130.2 %copy-start.23 = (bf16[256,256]{1,0:T(8,128)(2,1)}, bf16[256,256]{1,0:T(8,128)(2,1)S(1)}, u32[]{:S(2)}) copy-start(bf16[256,256]{1,0:T(8,128)(2,1)S(1)} %get-tuple-element.484) | copy-start | bytes 393220
  11.0 130.2 %copy-start.29 = (bf16[256,256]{1,0:T(8,128)(2,1)}, bf16[256,256]{1,0:T(8,128)(2,1)S(1)}, u32[]{:S(2)}) copy-start(bf16[256,256]{1,0:T(8,128)(2,1)S(1)} %get-tuple-element.488) | copy-start | bytes 393220
  11.0 130.2 %copy-start.31 = (bf16[256,256]{1,0:T(8,128)(2,1)}, bf16[256,256]{1,0:T(8,128)(2,1)S(1)}, u32[]{:S(2)}) copy-start(bf16[256,256]{1,0:T(8,128)(2,1)S(1)} %get-tuple-element.509) | copy-start | bytes 393220
  44.8 129.5 %copy-start.45 = (f32[1,256]{1,0:T(1,128)}, f32[1,256]{1,0:T(1,128)S(1)}, u32[]{:S(2)}) copy-start(f32[1,256]{1,0:T(1,128)S(1)} %get-tuple-element.499) | copy-start | bytes 3076
  90.8 46.9 %all-to-all-start = ((bf16[128,6,256]{2,1,0:T(8,128)(2,1)}), bf16[128,6,256]{2,1,0:T(8,128)(2,1)S(1)}, u32[]{:S(2)}, u32[]{:S(2)}) async-start(bf16[128,6,256]{2,1,0:T(8,128)(2,1)} %copy.103), calls=%async_computation | async-start | bytes 1048576 | tf_op jit(solution)/shard_map/all_to_all | solution.py:173
  117.1 138.4 %reduce-scatter.13.cloned.1.call-start = ((), (), s32[]{:S(2)}) async-start(), calls=%async_computation.18 | async-start | bytes 327680
  172.9 70.7 %copy-start.5 = (f32[128,1024]{1,0:T(8,128)}, f32[128,1024]{1,0:T(8,128)S(1)}, u32[]{:S(2)}) copy-start(f32[128,1024]{1,0:T(8,128)S(1)} %fusion.121) | copy-start | bytes 1572868
  230.8 8.7 %all-to-all-start.9 = ((bf16[4,64,256]{2,1,0:T(8,128)(2,1)}), bf16[4,64,256]{2,1,0:T(8,128)(2,1)S(1)}, u32[]{:S(2)}, u32[]{:S(2)}) async-start(bf16[4,64,256]{2,1,0:T(8,128)(2,1)} %convolution_convert_fusion.10), calls=%async_computation.9 | async-start | bytes 262144 | tf_op jit(solution)/shard_map/all_to_all | solution.py:410
  234.7 45.8 %reduce-scatter.15.cloned.1.call-start = ((), (), s32[]{:S(2)}) async-start(), calls=%async_computation.19 | async-start | bytes 327680
  239.6 11.6 %all-to-all-start.11 = ((bf16[4,64,1024]{2,1,0:T(8,128)(2,1)}), bf16[4,64,1024]{2,1,0:T(8,128)(2,1)S(1)}, u32[]{:S(2)}, u32[]{:S(2)}) async-start(bf16[4,64,1024]{2,1,0:T(8,128)(2,1)} %bitcast.113), calls=%async_computation.11 | async-start | bytes 1048576 | tf_op jit(solution)/shard_map/all_to_all | solution.py:413
  251.2 68.1 %all-to-all-start.13 = ((bf16[4,256,256]{2,1,0:T(8,128)(2,1)}), bf16[4,256,256]{2,1,0:T(8,128)(2,1)S(1)}, u32[]{:S(2)}, u32[]{:S(2)}) async-start(bf16[4,256,256]{2,1,0:T(8,128)(2,1)} %bitcast.417), calls=%async_computation.13 | async-start | bytes 1048576 | tf_op jit(solution)/shard_map/all_to_all | solution.py:416
  319.3 39.9 %all-to-all-start.1 = ((bf16[128,6,256]{2,1,0:T(8,128)(2,1)}), bf16[128,6,256]{2,1,0:T(8,128)(2,1)S(1)}, u32[]{:S(2)}, u32[]{:S(2)}) async-start(bf16[128,6,256]{2,1,0:T(8,128)(2,1)} %copy.117), calls=%async_computation.1 | async-start | bytes 1048576 | tf_op jit(solution)/shard_map/all_to_all | solution.py:173
  359.2 9.1 %all-to-all-start.7 = ((bf16[4,64,256]{2,1,0:T(8,128)(2,1)}), bf16[4,64,256]{2,1,0:T(8,128)(2,1)S(1)}, u32[]{:S(2)}, u32[]{:S(2)}) async-start(bf16[4,64,256]{2,1,0:T(8,128)(2,1)} %bitcast.97), calls=%async_computation.7 | async-start | bytes 262144 | tf_op jit(solution)/shard_map/all_to_all | solution.py:407
  368.4 70.4 %all-to-all-start.5 = ((bf16[4,64,256]{2,1,0:T(8,128)(2,1)}), bf16[4,64,256]{2,1,0:T(8,128)(2,1)S(1)}, u32[]{:S(2)}, u32[]{:S(2)}) async-start(bf16[4,64,256]{2,1,0:T(8,128)(2,1)} %bitcast.93), calls=%async_computation.5 | async-start | bytes 262144 | tf_op jit(solution)/shard_map/all_to_all | solution.py:404
  438.8 9.1 %all-to-all-start.3 = ((bf16[4,64,256]{2,1,0:T(8,128)(2,1)}), bf16[4,64,256]{2,1,0:T(8,128)(2,1)S(1)}, u32[]{:S(2)}, u32[]{:S(2)}) async-start(bf16[4,64,256]{2,1,0:T(8,128)(2,1)} %convolution_convert_fusion.16), calls=%async_computation.3 | async-start | bytes 262144 | tf_op jit(solution)/shard_map/all_to_all | solution.py:401
  447.8 8.1 %all-to-all-start.8 = ((bf16[4,64,256]{2,1,0:T(8,128)(2,1)}), bf16[4,64,256]{2,1,0:T(8,128)(2,1)S(1)}, u32[]{:S(2)}, u32[]{:S(2)}) async-start(bf16[4,64,256]{2,1,0:T(8,128)(2,1)} %convolution_convert_fusion.11), calls=%async_computation.8 | async-start | bytes 262144 | tf_op jit(solution)/shard_map/all_to_all | solution.py:392
  456.0 8.1 %all-to-all-start.2 = ((bf16[4,64,256]{2,1,0:T(8,128)(2,1)}), bf16[4,64,256]{2,1,0:T(8,128)(2,1)S(1)}, u32[]{:S(2)}, u32[]{:S(2)}) async-start(bf16[4,64,256]{2,1,0:T(8,128)(2,1)} %convolution_convert_fusion.17), calls=%async_computation.2 | async-start | bytes 262144 | tf_op jit(solution)/shard_map/all_to_all | solution.py:383
  459.3 26.7 %reduce-scatter.17.cloned.1.call-start = ((), (), s32[]{:S(2)}) async-start(), calls=%async_computation.20 | async-start | bytes 327680
  464.1 10.4 %all-to-all-start.10 = ((bf16[4,64,1024]{2,1,0:T(8,128)(2,1)}), bf16[4,64,1024]{2,1,0:T(8,128)(2,1)S(1)}, u32[]{:S(2)}, u32[]{:S(2)}) async-start(bf16[4,64,1024]{2,1,0:T(8,128)(2,1)} %bitcast.111), calls=%async_computation.10 | async-start | bytes 1048576 | tf_op jit(solution)/shard_map/all_to_all | solution.py:395
  474.5 10.8 %all-to-all-start.12 = ((bf16[4,256,256]{2,1,0:T(8,128)(2,1)}), bf16[4,256,256]{2,1,0:T(8,128)(2,1)S(1)}, u32[]{:S(2)}, u32[]{:S(2)}) async-start(bf16[4,256,256]{2,1,0:T(8,128)(2,1)} %bitcast.115), calls=%async_computation.12 | async-start | bytes 1048576 | tf_op jit(solution)/shard_map/all_to_all | solution.py:398
  478.0 34.3 %reduce-scatter.19.cloned.1.call-start = ((), (), s32[]{:S(2)}) async-start(), calls=%async_computation.21 | async-start | bytes 327680
  487.8 26.2 %all-to-all-start.4 = ((bf16[4,64,256]{2,1,0:T(8,128)(2,1)}), bf16[4,64,256]{2,1,0:T(8,128)(2,1)S(1)}, u32[]{:S(2)}, u32[]{:S(2)}) async-start(bf16[4,64,256]{2,1,0:T(8,128)(2,1)} %bitcast.91), calls=%async_computation.4 | async-start | bytes 262144 | tf_op jit(solution)/shard_map/all_to_all | solution.py:386
  514.1 8.1 %all-to-all-start.6 = ((bf16[4,64,256]{2,1,0:T(8,128)(2,1)}), bf16[4,64,256]{2,1,0:T(8,128)(2,1)S(1)}, u32[]{:S(2)}, u32[]{:S(2)}) async-start(bf16[4,64,256]{2,1,0:T(8,128)(2,1)} %bitcast.95), calls=%async_computation.6 | async-start | bytes 262144 | tf_op jit(solution)/shard_map/all_to_all | solution.py:389
  517.4 212.8 %all-reduce.4.cloned.1.call-start = ((), (), s32[]{:S(2)}) async-start(), calls=%async_computation.22 | async-start | bytes 3145728 | tf_op jit(solution)/shard_map/psum | solution.py:421
  (106 other events, 229.6 us)
Sparse Core Ops, SparseCore 0:
  230.1 22.4 reduce-scatter.12
  255.6 24.8 reduce-scatter.14
  462.9 21.0 reduce-scatter.16
  487.5 24.7 reduce-scatter.18
  523.4 206.7 all-reduce.3
where the time goes:
time: 754 us; the launch traced here: 743 us
  waiting for transfers between devices  205 us (27%)
  blocking collectives  159 us (21%)
  matrix products  144 us (19%)
  local copies, waits for them, and re-layouts  91.2 us (12%)
  starting transfers between devices  89 us (12%)
  other arithmetic  38.6 us (5%)
  between operations  15.1 us (2%)
    psum x1, waiting for transfers between devices, body(): lax.psum((uq, uk, uv, uo, uu, ud, tq, tk, tv, to_sum, tu, td), 'patch')  101 us
    psum x1, blocking collectives, body(): lax.psum((jnp.stack([first_gains[0], second_gains[0]]), jnp.stack([first_...  101 us
    scatter x4, local copies, waits for them, and re-layouts, ship_rows(): buffer_rows = buffer_rows.at[pack_owner, pack_slot].set(full_rows)  52.6 us
    all_to_all x2, starting transfers between devices, ship_rows(): lax.all_to_all(buffer_rows, 'patch', split_axis=0, concat_axis=0, tiled=T...  45.7 us
    unnamed x9, waiting for transfers between devices  45.3 us
    dot_general x32, matrix products, one_head(): jnp.einsum('npd,nkd->npk', grad_head, value_head, preferred_element_type=...  32.8 us
    dot_general x64, matrix products, head_probability(): jnp.einsum('npd,nkd->npk', query_head, key_head, preferred_element_type=j...  32.8 us
    all_to_all x2, waiting for transfers between devices, ship_rows(): lax.all_to_all(buffer_rows, 'patch', split_axis=0, concat_axis=0, tiled=T...  28.2 us
  transfers between devices with their start and end apart: 19, of which 13 were waited for; matrix products, arithmetic and copies ran while one was open for 18% of the time, Pallas kernels for 0%

commit v1 on v0

v1 whole, which is shorter than its diff:
```python
import functools

import jax
import jax.numpy as jnp
from jax import lax
from jax.experimental import pallas as pl
from jax.experimental.pallas import tpu as pltpu
from jax.sharding import PartitionSpec as P

HEADS = 16
PATCH = 512
HEAD_DIM = 16
WIDTH = 256
HIDDEN = 1024
SLOTS = 8

EPSILON = 1e-05
GELU_SCALE = 0.7978845608028654
GELU_CUBIC = 0.044715

BF = jnp.bfloat16
F32 = jnp.float32


def dot(left, right, left_dim=1, right_dim=0):
    return lax.dot_general(
        left, right, (((left_dim,), (right_dim,)), ((), ())), preferred_element_type=F32
    )


def norm_rows(values, gain_row):
    widened = values.astype(F32)
    centered = widened - jnp.mean(widened, axis=1, keepdims=True)
    inverse = lax.rsqrt(jnp.mean(centered * centered, axis=1, keepdims=True) + EPSILON)
    normed = centered * inverse
    return normed, inverse, (normed * gain_row).astype(BF)


def norm_back(grad_scaled, normed, inverse, gain_row):
    grad_normed = grad_scaled * gain_row
    centered = grad_normed - jnp.mean(grad_normed, axis=1, keepdims=True)
    return inverse * (centered - normed * jnp.mean(grad_normed * normed, axis=1, keepdims=True))


def gelu(pre):
    tangent = jnp.tanh(GELU_SCALE * (pre + GELU_CUBIC * (pre * pre * pre)))
    return 0.5 * pre * (1.0 + tangent)


def gelu_pair(pre):
    squared = pre * pre
    tangent = jnp.tanh(GELU_SCALE * (pre + GELU_CUBIC * (squared * pre)))
    half = 0.5 * (1.0 + tangent)
    slopes = half + 0.5 * pre * (1.0 - tangent * tangent) * (
        GELU_SCALE + GELU_SCALE * 3.0 * GELU_CUBIC * squared
    )
    return pre * half, slopes


def flip(values):
    return values.astype(F32).T.astype(BF)


def head_rows(head):
    return pl.ds(pl.multiple_of(head * HEAD_DIM, HEAD_DIM), HEAD_DIM)


def fill_bias(live_column, bias_ref):
    keys = lax.broadcasted_iota(jnp.int32, (PATCH, PATCH), 0)
    queries = lax.broadcasted_iota(jnp.int32, (PATCH, PATCH), 1)
    allowed = (live_column > 0) | (keys == queries)
    bias_ref[...] = jnp.where(allowed, 0.0, -1e30)


def attend(query, key, value, s):
    for head in range(HEADS):
        s.key_heads[head] = key[:, head * HEAD_DIM : (head + 1) * HEAD_DIM]
    s.query_t[...] = (query.astype(F32) * HEAD_DIM ** (-0.5)).T.astype(BF)
    s.value_t[...] = flip(value)

    def one_head(head, carry):
        rows = head_rows(head)
        scores = dot(s.key_heads[head], s.query_t[rows, :])
        weights = jnp.exp(scores + s.bias[...])
        inverse = 1.0 / jnp.sum(weights, axis=0, keepdims=True)
        s.inverse_sum[head] = inverse
        probability = (weights * inverse).astype(BF)
        s.heads_t[rows, :] = dot(s.value_t[rows, :], probability).astype(BF)
        return carry

    lax.fori_loop(0, HEADS, one_head, 0, unroll=2)


def attend_back(key, value, grad_heads, s):
    for head in range(HEADS):
        s.value_heads[head] = value[:, head * HEAD_DIM : (head + 1) * HEAD_DIM]
    s.key_t[...] = flip(key)
    s.grad_heads_t[...] = flip(grad_heads)

    def one_head(head, carry):
        rows = head_rows(head)
        query_rows = s.query_t[rows, :]
        grad_rows = s.grad_heads_t[rows, :]
        scores = dot(s.key_heads[head], query_rows)
        probability = jnp.exp(scores + s.bias[...]) * s.inverse_sum[head]
        grad_wide = grad_rows.astype(F32) * HEAD_DIM ** (-0.5)
        inner = jnp.sum(grad_wide * s.heads_t[rows, :].astype(F32), axis=0, keepdims=True)
        grad_prob = dot(s.value_heads[head], grad_wide.astype(BF))
        grad_score = (probability * (grad_prob - inner)).astype(BF)
        s.grad_value_t[rows, :] = dot(grad_rows, probability.astype(BF), 1, 1).astype(BF)
        s.grad_query_t[rows, :] = dot(s.key_t[rows, :], grad_score).astype(BF)
        s.grad_key_t[rows, :] = (
            dot(query_rows, grad_score, 1, 1) * HEAD_DIM**0.5
        ).astype(BF)
        return carry

    lax.fori_loop(0, HEADS, one_head, 0, unroll=2)


def feed_forward(middle, up_weight, gain_feed):
    normed_m, inverse_m, scaled_m = norm_rows(middle, gain_feed)
    return normed_m, inverse_m, scaled_m, dot(scaled_m, up_weight)


def backward(part, grad_rows, x, middle, key, value, w, s, out, want_grad_in):
    normed_m, inverse_m, scaled_m, pre = feed_forward(middle, w.up[...], w.gain_feed[...])
    activated, slopes = gelu_pair(pre)
    s.hidden[...] = activated.astype(BF)
    s.turned[...] = flip(scaled_m)
    quarter = pl.ds(pl.multiple_of(part * (WIDTH // 4), WIDTH // 4), WIDTH // 4)
    hidden_part = s.hidden[:, pl.ds(pl.multiple_of(part * WIDTH, WIDTH), WIDTH)]
    out[512:768, :] = dot(hidden_part, grad_rows, 0, 0).astype(out.dtype)
    grad_pre = (dot(grad_rows, w.down[...], 1, 1) * slopes).astype(BF)
    up_grad = dot(s.turned[quarter, :], grad_pre)
    for piece in range(4):
        out[256 + 64 * piece : 320 + 64 * piece, :] = up_grad[
            :, WIDTH * piece : WIDTH * (piece + 1)
        ].astype(out.dtype)
    grad_scaled_m = dot(grad_pre, w.up[...], 1, 1)
    feed_gain = jnp.sum(grad_scaled_m * normed_m, axis=0, keepdims=True)
    grad_middle = (
        grad_rows.astype(F32)
        + norm_back(grad_scaled_m, normed_m, inverse_m, w.gain_feed[...])
    ).astype(BF)
    out[192:256, :] = dot(s.heads_t[quarter, :], grad_middle).astype(out.dtype)
    grad_heads = dot(grad_middle, w.out[...], 1, 1).astype(BF)
    attend_back(key, value, grad_heads, s)
    normed_a, inverse_a, scaled_a = norm_rows(x, w.gain_mixer[...])
    s.turned[...] = flip(scaled_a)
    scaled_part = s.turned[quarter, :]
    out[0:64, :] = dot(scaled_part, s.grad_query_t[...], 1, 1).astype(out.dtype)
    out[64:128, :] = dot(scaled_part, s.grad_key_t[...], 1, 1).astype(out.dtype)
    out[128:192, :] = dot(scaled_part, s.grad_value_t[...], 1, 1).astype(out.dtype)
    grad_scaled_a = (
        dot(w.query[...], s.grad_query_t[...])
        + dot(w.key[...], s.grad_key_t[...])
        + dot(w.value[...], s.grad_value_t[...])
    ).T
    mixer_gain = jnp.sum(grad_scaled_a * normed_a, axis=0, keepdims=True)
    gains = jnp.concatenate([mixer_gain, feed_gain, jnp.zeros((14, WIDTH), F32)], axis=0)
    out[768:784, :] = gains.astype(out.dtype)
    out[784:, :] = jnp.zeros((out.shape[0] - 784, WIDTH), out.dtype)
    if not want_grad_in:
        return None
    return (
        grad_middle.astype(F32) + norm_back(grad_scaled_a, normed_a, inverse_a, w.gain_mixer[...])
    ).astype(BF)


class Named:
    def __init__(self, names, refs):
        for name, ref in zip(names, refs, strict=True):
            setattr(self, name, ref)


WEIGHTS = ("gain_mixer", "query", "key", "value", "out", "gain_feed", "up", "down")
FORWARD_SCRATCH = (
    ("key_heads", (HEADS, PATCH, HEAD_DIM), BF),
    ("query_t", (WIDTH, PATCH), BF),
    ("value_t", (WIDTH, PATCH), BF),
    ("bias", (PATCH, PATCH), F32),
    ("inverse_sum", (HEADS, 1, PATCH), F32),
    ("heads_t", (WIDTH, PATCH), BF),
)
BACKWARD_SCRATCH = (
    ("value_heads", (HEADS, PATCH, HEAD_DIM), BF),
    ("key_t", (WIDTH, PATCH), BF),
    ("grad_heads_t", (WIDTH, PATCH), BF),
    ("grad_query_t", (WIDTH, PATCH), BF),
    ("grad_key_t", (WIDTH, PATCH), BF),
    ("grad_value_t", (WIDTH, PATCH), BF),
    ("turned", (WIDTH, PATCH), BF),
    ("hidden", (PATCH, HIDDEN), BF),
)


def project(scaled, w, s):
    query = dot(scaled, w.query[...]).astype(BF)
    key = dot(scaled, w.key[...]).astype(BF)
    value = dot(scaled, w.value[...]).astype(BF)
    return query, key, value


def forward(x, live_column, w, s):
    fill_bias(live_column, s.bias)
    normed, inverse, scaled = norm_rows(x, w.gain_mixer[...])
    query, key, value = project(scaled, w, s)
    attend(query, key, value, s)
    heads_out = s.heads_t[...].astype(F32).T.astype(BF)
    middle = (x.astype(F32) + dot(heads_out, w.out[...])).astype(BF)
    return key, value, middle


def first_kernel(*refs):
    count_ref, x_ref, depart_ref = refs[:3]
    w = Named(WEIGHTS, refs[3:11])
    packed_ref, key_ref, value_ref, middle_ref, query_t_ref, heads_t_ref, inverse_ref = refs[11:18]
    s = Named(("key_heads", "value_t", "bias"), refs[18:21])
    s.query_t = query_t_ref
    s.heads_t = heads_t_ref
    s.inverse_sum = inverse_ref
    x = x_ref[...]
    live = (lax.broadcasted_iota(jnp.int32, (PATCH, 1), 0) < count_ref[0]).astype(jnp.int32)
    key, value, middle = forward(x, live, w, s)
    key_ref[...] = key
    value_ref[...] = value
    middle_ref[...] = middle
    _, _, _, pre = feed_forward(middle, w.up[...], w.gain_feed[...])
    block_out = (middle.astype(F32) + dot(gelu(pre).astype(BF), w.down[...])).astype(BF)
    places = lax.broadcasted_iota(jnp.int32, (packed_ref.shape[0], PATCH), 0)
    chosen = (places == depart_ref[...]).astype(BF)
    packed_ref[...] = dot(chosen, block_out).astype(BF)


def middle_kernel(*refs):
    part_ref, arrived_ref, live_ref, arrive_row_ref, arrive_column_ref, cotangent_ref = refs[:6]
    w = Named(WEIGHTS, refs[6:14])
    out_ref, grads_ref, packed_ref = refs[14:17]
    s = Named([name for name, _, _ in FORWARD_SCRATCH + BACKWARD_SCRATCH], refs[17:31])
    rows_ref = refs[31]
    part = part_ref[0]
    buffer_rows = arrived_ref.shape[0]
    columns = lax.broadcasted_iota(jnp.int32, (PATCH, buffer_rows), 1)
    chosen = (columns == arrive_column_ref[...]).astype(BF)
    x = dot(chosen, arrived_ref[...]).astype(BF)
    key, value, middle = forward(x, live_ref[...], w, s)
    own = pl.ds(pl.multiple_of(part * (PATCH // 4), PATCH // 4), PATCH // 4)
    rows_ref[...] = middle
    middle_part = rows_ref[own, :]
    _, _, _, pre = feed_forward(middle_part, w.up[...], w.gain_feed[...])
    out_ref[...] = (
        middle_part.astype(F32) + dot(gelu(pre).astype(BF), w.down[...])
    ).astype(BF)
    grad_in = backward(
        part, cotangent_ref[...], x, middle, key, value, w, s, grads_ref, True
    )
    places = lax.broadcasted_iota(jnp.int32, (buffer_rows, PATCH), 0)
    packed_ref[...] = dot((places == arrive_row_ref[...]).astype(BF), grad_in).astype(BF)


def last_kernel(*refs):
    part_ref, count_ref, arrived_ref, depart_column_ref, x_ref = refs[:5]
    key_ref, value_ref, middle_ref, query_t_ref, heads_t_ref, inverse_ref = refs[5:11]
    w = Named(WEIGHTS, refs[11:19])
    grads_ref = refs[19]
    s = Named(
        [name for name, _, _ in FORWARD_SCRATCH[:1] + FORWARD_SCRATCH[3:4] + BACKWARD_SCRATCH],
        refs[20:30],
    )
    s.query_t = query_t_ref
    s.heads_t = heads_t_ref
    s.inverse_sum = inverse_ref
    live = (lax.broadcasted_iota(jnp.int32, (PATCH, 1), 0) < count_ref[0]).astype(jnp.int32)
    fill_bias(live, s.bias)
    columns = lax.broadcasted_iota(jnp.int32, (PATCH, arrived_ref.shape[0]), 1)
    chosen = (columns == depart_column_ref[...]).astype(BF)
    grad_rows = dot(chosen, arrived_ref[...]).astype(BF)
    key = key_ref[...]
    for head in range(HEADS):
        s.key_heads[head] = key[:, head * HEAD_DIM : (head + 1) * HEAD_DIM]
    backward(
        part_ref[0], grad_rows, x_ref[...], middle_ref[...], key, value_ref[...], w, s,
        grads_ref, False,
    )


def whole(array):
    zeros = (0,) * array.ndim
    return pl.BlockSpec(array.shape, lambda step: zeros)


def weight_spec(array, block):
    zeros = (0,) * (array.ndim - 1)
    return pl.BlockSpec((None,) + array.shape[1:], lambda step: (block,) + zeros)


def call(kernel, scalars, arrays, weights, block, out_shapes, scratch, name):
    return pl.pallas_call(
        kernel,
        grid=(1,),
        out_shape=out_shapes,
        in_specs=[pl.BlockSpec(memory_space=pltpu.SMEM) for _ in scalars]
        + [whole(array) for array in arrays]
        + [weight_spec(array, block) for array in weights],
        out_specs=jax.tree.map(whole, out_shapes),
        scratch_shapes=[pltpu.VMEM(shape, dtype) for _, shape, dtype in scratch],
        compiler_params=pltpu.CompilerParams(vmem_limit_bytes=56 * 1024 * 1024),
        name=name,
    )(*scalars, *arrays, *weights)


def exchange(buffer):
    return lax.all_to_all(buffer, "patch", split_axis=0, concat_axis=0, tiled=True)


def fold(terms):
    shaped = terms.reshape(terms.shape[0] // SLOTS, SLOTS, WIDTH)
    return jnp.sum(shaped.astype(F32), axis=0).astype(BF)


def body(
    points,
    patch_counts,
    to_hilbert,
    from_hilbert,
    cotangent,
    gain_mixer,
    query_weight,
    key_weight,
    value_weight,
    out_weight,
    gain_feed,
    up_weight,
    down_weight,
):
    peer_count = lax.axis_size("patch")
    buffer_rows = peer_count * SLOTS
    part = lax.axis_index("mp").astype(jnp.int32).reshape(1)
    count = lax.dynamic_slice_in_dim(patch_counts, lax.axis_index("patch"), 1, 0)
    position = jnp.arange(PATCH, dtype=jnp.int32)

    def places(owners, ranking):
        ahead = (owners[:, None] == owners[None, :]) & (ranking[None, :] < ranking[:, None])
        return owners * SLOTS + jnp.sum(ahead.astype(jnp.int32), axis=1)

    depart = places(to_hilbert // PATCH, position)
    arrive = places(from_hilbert // PATCH, from_hilbert)
    source_patch = from_hilbert // PATCH
    source_count = jnp.sum(
        jnp.where(
            source_patch[:, None] == jnp.arange(peer_count, dtype=jnp.int32)[None, :],
            patch_counts[None, :],
            0,
        ),
        axis=1,
    )
    live_hilbert = (from_hilbert % PATCH < source_count).astype(jnp.int32)
    weights = (
        gain_mixer[:, None, :],
        query_weight,
        key_weight,
        value_weight,
        out_weight,
        gain_feed[:, None, :],
        up_weight,
        down_weight,
    )
    rows = jax.ShapeDtypeStruct((PATCH, WIDTH), BF)
    turned = jax.ShapeDtypeStruct((WIDTH, PATCH), BF)
    packed = jax.ShapeDtypeStruct((buffer_rows, WIDTH), BF)
    x = lax.all_gather(points, "mp", axis=0, tiled=True)
    cotangent_rows = lax.all_gather(cotangent, "mp", axis=0, tiled=True)
    sent, key, value, middle, query_t, heads_t, inverse = call(
        first_kernel,
        (count,),
        (x, depart[None, :]),
        weights,
        0,
        (
            packed,
            rows,
            rows,
            rows,
            turned,
            turned,
            jax.ShapeDtypeStruct((HEADS, 1, PATCH), F32),
        ),
        (FORWARD_SCRATCH[0], FORWARD_SCRATCH[2], FORWARD_SCRATCH[3]),
        "first_block",
    )
    arrived = exchange(sent)
    hilbert_out, second_grads, grad_sent = call(
        middle_kernel,
        (part,),
        (arrived, live_hilbert[:, None], arrive[None, :], arrive[:, None], cotangent_rows),
        weights,
        1,
        (jax.ShapeDtypeStruct((PATCH // 4, WIDTH), BF), packed, packed),
        FORWARD_SCRATCH + BACKWARD_SCRATCH + (("rows", (PATCH, WIDTH), BF),),
        "second_block",
    )
    grad_arrived = exchange(grad_sent)
    first_grads = call(
        last_kernel,
        (part, count),
        (grad_arrived, depart[:, None], x, key, value, middle, query_t, heads_t, inverse),
        weights,
        0,
        packed,
        (FORWARD_SCRATCH[0], FORWARD_SCRATCH[3]) + BACKWARD_SCRATCH,
        "first_block_back",
    )
    second_terms = exchange(second_grads)
    first_terms = exchange(first_grads)
    own_sums = jnp.concatenate([fold(first_terms), fold(second_terms)], axis=0)
    spread = jnp.broadcast_to(own_sums[None], (peer_count,) + own_sums.shape)
    both = lax.all_to_all(spread, "patch", split_axis=0, concat_axis=0, tiled=True)
    both = both.reshape(peer_count, 2, SLOTS, WIDTH).transpose(1, 0, 2, 3)
    both = both.reshape(2, buffer_rows, WIDTH).astype(F32)
    up_grad = both[:, 256:512].reshape(2, 4, 64, WIDTH).transpose(0, 2, 1, 3).reshape(2, 64, HIDDEN)
    return (
        hilbert_out,
        both[:, 768],
        both[:, 0:64],
        both[:, 64:128],
        both[:, 128:192],
        both[:, 192:256],
        both[:, 769],
        up_grad,
        both[:, 512:768],
    )


def solution(mesh):
    split = P(("patch", "mp"), None)
    in_specs = (split, P(), P("patch"), P("patch"), split) + (P(),) * 8
    own_rows = P(None, "mp", None)
    out_specs = (split, P(), own_rows, own_rows, own_rows, own_rows, P(), own_rows, own_rows)
    return jax.shard_map(body, mesh=mesh, in_specs=in_specs, out_specs=out_specs, check_vma=False)
```

time: 754 us -> 229 us (0.30); the launches traced: 743 us -> 229 us
  waiting for transfers between devices: 205 us -> 29.4 us
  matrix products: 144 us -> 0 us
  local copies, waits for them, and re-layouts: 91.2 us -> 10.3 us
  blocking collectives: 159 us -> 89.2 us
  Pallas kernels: 0 us -> 58.3 us
  starting transfers between devices: 89 us -> 37.4 us
  other arithmetic: 38.6 us -> 3.27 us
  between operations: 15.1 us -> 0.74 us
    dot_general x252 -> x0, matrix products: 144 us -> none  [the longest x32 32.8 us: one_head(): jnp.einsum('npd,nkd->npk', grad_head, value_head, preferred_element_type=...]
    psum x1 -> x0, waiting for transfers between devices: 101 us -> none  [body(): lax.psum((uq, uk, uv, uo, uu, ud, tq, tk, tv, to_sum, tu, td), 'patch')]
    psum x1 -> x0, blocking collectives: 101 us -> none  [body(): lax.psum((jnp.stack([first_gains[0], second_gains[0]]), jnp.stack([first_...]
    all_to_all x0 -> x2, blocking collectives: none -> 65.6 us  [the longest x1 36.1 us: body(): lax.all_to_all(spread, 'patch', split_axis=0, concat_axis=0, tiled=True)]
    pallas_call x0 -> x3, Pallas kernels: none -> 58.3 us  [call(): pl.pallas_call(kernel, grid=(1,), out_shape=out_shapes, in_specs=[pl.Bloc...]
    scatter x4 -> x0, local copies, waits for them, and re-layouts: 52.6 us -> none  [ship_rows(): buffer_rows = buffer_rows.at[pack_owner, pack_slot].set(full_rows)]
    all_to_all x14 -> x3, starting transfers between devices: 88.9 us -> 37.4 us  [exchange(): lax.all_to_all(buffer, 'patch', split_axis=0, concat_axis=0, tiled=True)]
    unnamed x9 -> x0, waiting for transfers between devices: 45.3 us -> none
  transfers between devices with their start and end apart: 19 -> 3, of which waited for: 13 -> 3; matrix products, arithmetic and copies ran while one was open for 18% -> 1% of each run, Pallas kernels for 0% -> 8%
where the time goes in v1:
time: 229 us
  blocking collectives  89.2 us (39%)
  Pallas kernels  58.3 us (25%)
  starting transfers between devices  37.4 us (16%)
  waiting for transfers between devices  29.4 us (13%)
  local copies, waits for them, and re-layouts  10.3 us (4%)
  other arithmetic  3.27 us (1%)
    pallas_call x3, Pallas kernels, call(): pl.pallas_call(kernel, grid=(1,), out_shape=out_shapes, in_specs=[pl.Bloc...  58.3 us
    all_to_all x3, starting transfers between devices, exchange(): lax.all_to_all(buffer, 'patch', split_axis=0, concat_axis=0, tiled=True)  37.4 us
    all_to_all x1, blocking collectives, body(): lax.all_to_all(spread, 'patch', split_axis=0, concat_axis=0, tiled=True)  36.1 us
    all_to_all x1, blocking collectives, exchange(): lax.all_to_all(buffer, 'patch', split_axis=0, concat_axis=0, tiled=True)  29.5 us
    all_to_all x3, waiting for transfers between devices, exchange(): lax.all_to_all(buffer, 'patch', split_axis=0, concat_axis=0, tiled=True)  29.4 us
    all_gather x1, blocking collectives, body(): x = lax.all_gather(points, 'mp', axis=0, tiled=True)  12.8 us
    all_gather x1, blocking collectives, body(): cotangent_rows = lax.all_gather(cotangent, 'mp', axis=0, tiled=True)  10.8 us
  transfers between devices with their start and end apart: 3, of which 3 were waited for; matrix products, arithmetic and copies ran while one was open for 1% of the time, Pallas kernels for 8%

profile of v1, /device:TPU:1, one launch (start us, length us, event | category | flops | bytes accessed | tf_op | source)
XLA Modules:
  0.0 228.6 jit_solution(5961006193478397990)
XLA Ops:
  0.6 1.3 broadcast_in_dim.53.refs_3_.refs_6_.refs_11_
  1.9 1.3 broadcast_in_dim.54.refs_8_.refs_11_.refs_16_
  3.2 12.8 %all_gather.6.refs_1_.refs_4_ = bf16[512,256]{1,0:T(8,128)(2,1)} all-gather(bf16[128,256]{1,0:T(8,128)(2,1)} %param.13), channel_id=1, replica_groups=mesh['patch'=128,'mp'=4] {'mp'}, dimensions={0}, use_global_device_ids=true | all-gather | bytes 327680 | tf_op jit(solution)/shard_map/all_gather | solution.py:371
  16.9 1.3 multiply_add_fusion.1
  18.2 1.2 dynamic_slice.3.refs_0_.refs_1_
  19.4 13.6 %first_block.1 = (bf16[1024,256]{1,0:T(8,128)(2,1)}, bf16[512,256]{1,0:T(8,128)(2,1)}, bf16[512,256]{1,0:T(8,128)(2,1)}, bf16[512,256]{1,0:T(8,128)(2,1)}, bf16[...) custom-call(s32[1]{0:T(128)} %dynamic_slice.3.refs_0_.refs_1_, ...), custom_call_target="tpu_custom_call" | custom-call | tf_op jit(solution)/shard_map/first_block/pallas_call | solution.py:298
  33.0 19.8 %all-to-all-start = ((bf16[128,8,256]{2,1,0:T(8,128)(2,1)}), bf16[128,8,256]{2,1,0:T(8,128)(2,1)S(1)}, u32[]{:S(2)}, u32[]{:S(2)}) async-start(bf16[128,8,256]{2,1,0:T(8,128)(2,1)} %bitcast.36), calls=%async_computation | async-start | bytes 1048576 | tf_op jit(solution)/shard_map/all_to_all | solution.py:313
  53.2 0.8 copy.33.refs_4_
  54.3 0.9 copy.32.refs_2_
  55.2 10.8 %all_gather.7.refs_5_ = bf16[512,256]{1,0:T(8,128)(2,1)} all-gather(bf16[128,256]{1,0:T(8,128)(2,1)S(1)} %copy-done.1), channel_id=1, replica_groups=mesh['patch'=128,'mp'=4] {'mp'}, dimensions={0}, use_global_device_ids=true | all-gather | bytes 327680 | tf_op jit(solution)/shard_map/all_gather | solution.py:372
  66.0 7.4 %all-to-all-done = bf16[128,8,256]{2,1,0:T(8,128)(2,1)S(1)} async-done(((bf16[128,8,256]{2,1,0:T(8,128)(2,1)}), bf16[128,8,256]{2,1,0:T(8,128)(2,1)S(1)}, u32[]{:S(2)}, u32[]{:S(2)}) %all-to-all-start) | async-done | bytes 524320 | tf_op jit(solution)/shard_map/all_to_all | solution.py:313
  73.4 0.8 copy-done
  74.2 26.7 %second_block.1 = (bf16[128,256]{1,0:T(8,128)(2,1)}, bf16[1024,256]{1,0:T(8,128)(2,1)}, bf16[1024,256]{1,0:T(8,128)(2,1)}) custom-call(s32[1]{0:T(128)} %bitcast.refs_0_, bf16[1024,256]{1,0:T(8,128)(2,1)} %bitcast.30, s32[512,1]{1,0:T(8,128)} %copy.32.refs_2_, s32[1,512]{1,0:T(1,128)} %bitcast.39, s32[512,1]{1,0:T(8,128)} %copy.33.refs_4_, ...), custom_call_target="tpu_custom_call" | custom-call | tf_op jit(solution)/shard_map/second_block/pallas_call | solution.py:298
  100.9 29.5 %all_to_all.45 = bf16[128,8,256]{2,1,0:T(8,128)(2,1)} all-to-all(bf16[128,8,256]{2,1,0:T(8,128)(2,1)} %bitcast.37), channel_id=1, replica_groups=mesh['patch'=128,'mp'=4] {'patch'}, dimensions={0} | all-to-all | bytes 1048576 | tf_op jit(solution)/shard_map/all_to_all | solution.py:313
  130.4 5.5 %all-to-all-start.3 = ((bf16[128,8,256]{2,1,0:T(8,128)(2,1)}), bf16[128,8,256]{2,1,0:T(8,128)(2,1)S(1)}, u32[]{:S(2)}, u32[]{:S(2)}) async-start(bf16[128,8,256]{2,1,0:T(8,128)(2,1)} %bitcast.34), calls=%async_computation.3 | async-start | bytes 1048576 | tf_op jit(solution)/shard_map/all_to_all | solution.py:313
  136.0 0.8 copy.34.refs_3_
  136.8 18.0 %first_block_back.1 = bf16[1024,256]{1,0:T(8,128)(2,1)} custom-call(s32[1]{0:T(128)} %bitcast.refs_0_, s32[1]{0:T(128)} %dynamic_slice.3.refs_0_.refs_1_, bf16[1024,256]{1,0:T(8,128)(2,1)} %bitcast.32, s32[512,1]{1,0:T(8,128)} %copy.34.refs_3_, bf16[512,256]{1,0:T(8,128)(2,1)} %all_gather.6.refs_1_.refs_4_, bf16[512,256]{1,0:T(8,128)(2,1)} %get-tuple-element.22.refs_5_, ...), custom_call_target="tpu_custom_call" | custom-call | tf_op jit(solution)/shard_map/first_block_back/pallas_call | solution.py:298
  154.8 1.6 all-to-all-done.3
  156.4 12.0 %all-to-all-start.2 = ((bf16[128,8,256]{2,1,0:T(8,128)(2,1)}), bf16[128,8,256]{2,1,0:T(8,128)(2,1)S(1)}, u32[]{:S(2)}, u32[]{:S(2)}) async-start(bf16[128,8,256]{2,1,0:T(8,128)(2,1)} %bitcast.31), calls=%async_computation.2 | async-start | bytes 1048576 | tf_op jit(solution)/shard_map/all_to_all | solution.py:313
  168.6 20.4 %all-to-all-done.2 = bf16[128,8,256]{2,1,0:T(8,128)(2,1)S(1)} async-done(((bf16[128,8,256]{2,1,0:T(8,128)(2,1)}), bf16[128,8,256]{2,1,0:T(8,128)(2,1)S(1)}, u32[]{:S(2)}, u32[]{:S(2)}) %all-to-all-start.2) | async-done | bytes 524320 | tf_op jit(solution)/shard_map/all_to_all | solution.py:313
  189.3 36.1 %all_to_all.46 = bf16[128,16,256]{2,1,0:T(8,128)(2,1)S(1)} all-to-all(bf16[128,16,256]{2,1,0:T(8,128)(2,1)S(1)} %broadcast_in_dim.62), channel_id=1, replica_groups=mesh['patch'=128,'mp'=4] {'patch'}, dimensions={0} | all-to-all | bytes 2097152 | tf_op jit(solution)/shard_map/all_to_all | solution.py:417
  225.5 0.9 fusion.6
  226.4 0.8 fusion.8
  227.2 0.9 copy.39
  (25 shorter events, 2.7 us)
Async XLA Ops:
  19.4 33.4 %copy-start.2 = (s32[512]{0:T(512)S(1)}, s32[512]{0:T(512)}, u32[]{:S(2)}) copy-start(s32[512]{0:T(512)} %param.16) | copy-start | bytes 6148
  19.4 34.7 %copy-start.5 = (s32[128]{0:T(128)S(1)}, s32[128]{0:T(128)}, u32[]{:S(2)}) copy-start(s32[128]{0:T(128)} %param.14) | copy-start | bytes 1540
  19.4 35.8 %copy-start.1 = (bf16[128,256]{1,0:T(8,128)(2,1)S(1)}, bf16[128,256]{1,0:T(8,128)(2,1)}, u32[]{:S(2)}) copy-start(bf16[128,256]{1,0:T(8,128)(2,1)} %param.17) | copy-start | bytes 196612
  33.0 40.4 %all-to-all-start = ((bf16[128,8,256]{2,1,0:T(8,128)(2,1)}), bf16[128,8,256]{2,1,0:T(8,128)(2,1)S(1)}, u32[]{:S(2)}, u32[]{:S(2)}) async-start(bf16[128,8,256]{2,1,0:T(8,128)(2,1)} %bitcast.36), calls=%async_computation | async-start | bytes 1048576 | tf_op jit(solution)/shard_map/all_to_all | solution.py:313
  53.2 20.2 %copy-start.3 = (s32[512]{0:T(512)}, s32[512]{0:T(512)S(1)}, u32[]{:S(2)}) copy-start(s32[512]{0:T(512)S(1)} %multiply_add_fusion) | copy-start | bytes 6148
  73.4 0.8 copy-start
  100.9 35.0 %copy-start.4 = (s32[512]{0:T(512)S(1)}, s32[512]{0:T(512)}, u32[]{:S(2)}) copy-start(s32[512]{0:T(512)} %multiply_add_fusion.1) | copy-start | bytes 6148
  130.4 26.0 %all-to-all-start.3 = ((bf16[128,8,256]{2,1,0:T(8,128)(2,1)}), bf16[128,8,256]{2,1,0:T(8,128)(2,1)S(1)}, u32[]{:S(2)}, u32[]{:S(2)}) async-start(bf16[128,8,256]{2,1,0:T(8,128)(2,1)} %bitcast.34), calls=%async_computation.3 | async-start | bytes 1048576 | tf_op jit(solution)/shard_map/all_to_all | solution.py:313
  156.4 32.6 %all-to-all-start.2 = ((bf16[128,8,256]{2,1,0:T(8,128)(2,1)}), bf16[128,8,256]{2,1,0:T(8,128)(2,1)S(1)}, u32[]{:S(2)}, u32[]{:S(2)}) async-start(bf16[128,8,256]{2,1,0:T(8,128)(2,1)} %bitcast.31), calls=%async_computation.2 | async-start | bytes 1048576 | tf_op jit(solution)/shard_map/all_to_all | solution.py:313
